TPU v7x, 32 devices: a whole 2x2x4 slice. The times are simulated.
32 devices in a mesh: src: 4 (over z), tgt: 8 (over y, x, core).
Axes of the slice: x: 2, y: 2, z: 4, core: 2. Of those that a mesh axis runs over, the one named last changes fastest.
Arguments:
- src_points: bfloat16 [32, 256, 128], P('src', 'tgt')
- tgt_points: bfloat16 [64, 256, 128], P('tgt', 'src'), may hold values from -1.5 to 1.5
- src_mass: bfloat16 [32, 256], P('src', 'tgt'), may hold values from 0.099609375 to 10
- tgt_mass: bfloat16 [64, 256], P('tgt', 'src'), may hold values from 0.099609375 to 10
- src_potential: bfloat16 [32, 256], P('src', 'tgt'), may hold values from -452 to 452
- tgt_potential: bfloat16 [64, 256], P('tgt', 'src'), may hold values from -452 to 452
- src_counts: int32 [32], P('src'), may hold values from 16 to 256, as said below
- tgt_counts: int32 [64], P('tgt'), may hold values from 16 to 256, as said below
- keep: int32 [32, 64], P('src', 'tgt'), may hold values from 0 to 1, as said below
Outputs:
- images: float32 [32, 256, 128], P('src', 'tgt')
- src_final: float32 [32, 256], P('src', 'tgt')
- tgt_final: float32 [64, 256], P('tgt', 'src')
Inputs may be any that keep to these rules, and one draw needn't show every extreme that they name: `keep`: every source block keeps at least one target block and every target block is kept by at least one source block. `src_counts`: some source block is full. `tgt_counts`: some target block is full.
All inputs are finite; a program needn't handle non-finite values.
Results may differ from a plain program's by a relative error of at most 0.0003.
Values may be sent and summed in bfloat16 or wider, within the bound.
No kernel may reach another device: no remote copies, remote signals or barrier semaphores. Data moves between devices by JAX's collectives and lax.ppermute only.
A program may use at most 64 MiB of HBM per device.

v0:
```python
import functools
import math

import jax
import jax.numpy as jnp
from jax import lax
from jax.experimental import pallas as pl
from jax.experimental.pallas import tpu as pltpu
from jax.sharding import PartitionSpec as P

ITERS = 4
EPSILON = 0.1
UNIT = 1.0 / (EPSILON * math.log(2.0))
FLOOR = -1e30
LANES = 128
FAR = (0, 1, 3, 2)
GROUP = 16
MOVE_GROUP = 6

SMEM = pl.BlockSpec(memory_space=pltpu.SMEM)
VMEM = pl.BlockSpec(memory_space=pltpu.VMEM)
PARAMS = pltpu.CompilerParams(vmem_limit_bytes=40 * 1024 * 1024)


def f32(*shape):
    return jax.ShapeDtypeStruct(shape, jnp.float32)


def swap(part, axis, mask):
    return lax.ppermute(part, axis, [(i, i ^ mask) for i in range(lax.axis_size(axis))])


def near_count(axis):
    return lax.axis_size(axis) // 4


def merge_lse(parts):
    top = functools.reduce(jnp.maximum, parts)
    return top + jnp.log2(sum(jnp.exp2(part - top) for part in parts))


def exchange_lse(part, axis):
    near = near_count(axis)
    if near > 1:
        part = merge_lse([part] + [swap(part, axis, d) for d in range(1, near)])
    return [part] + [swap(part, axis, near * k) for k in range(1, 4)]


def shared_rows():
    return near_count("tgt") == 2 and near_count("src") == 1


def is_odd():
    return lax.rem(lax.axis_index("tgt"), 2) == 1


def exchange_plain(part, sb):
    return jnp.concatenate([merge_lse(exchange_lse(part[:sb], "tgt")), merge_lse(exchange_lse(part[sb:], "src"))])


def exchange_first(part, sb):
    other = swap(part, "tgt", 1)
    rows = merge_lse([part[:sb], other[:sb]])
    part = jnp.where(is_odd(), padded(rows, part), jnp.concatenate([part[sb:], other[sb:]]))
    return exchange_shared(part, 1)


def padded(rows, part):
    return jnp.concatenate([rows] * (part.shape[0] // rows.shape[0]))


def exchange_shared(part, row_side):
    ntgt, nsrc = lax.axis_size("tgt"), lax.axis_size("src")

    def swap_far(k):
        pairs = [
            (s * ntgt + t, s * ntgt + (t ^ (2 * k)) if t % 2 == row_side else (s ^ FAR[k]) * ntgt + t)
            for s in range(nsrc)
            for t in range(ntgt)
        ]
        return lax.ppermute(part, ("src", "tgt"), pairs)

    return merge_lse([part] + [swap_far(k) for k in range(1, 4)])


def gather_points(x_piece, y_piece, y_rows):
    nx, ny = near_count("tgt"), near_count("src")
    y_two = swap(y_piece, "src", 2 * ny)
    y_one, y_three = swap(y_piece, "src", ny), swap(y_piece, "src", 3 * ny)
    x_far = [swap(x_piece, "tgt", nx * k) for k in range(1, 4)]
    y_one, y_three, *x_far = lax.optimization_barrier((y_one, y_three, *x_far))
    y_found = [(0, 0, y_piece), (ny, 0, y_one), (2 * ny, 0, y_two), (3 * ny, 0, y_three)]
    x_found = [(0, 0, x_piece)] + [(nx * k, 0, x_far[k - 1]) for k in range(1, 4)]
    return spread_near(x_found, "tgt"), spread_near(y_found, "src")


def spread_near(found, axis):
    near = near_count(axis)
    arrays, parts = [], []
    for d in range(near):
        for mask, first, array in found:
            parts.append((mask ^ d, first, len(arrays), array.shape[0]))
            arrays.append(swap(array, axis, d) if d else array)
    return arrays, parts


def whole_block(ref, k):
    piece = ref[:, k]
    return piece.reshape(piece.shape[0] * piece.shape[1], piece.shape[2])


def split_columns(vec, split_ref):
    blocks, slots = vec.shape
    vec = vec * (1.0 / UNIT)
    parts = []
    for _ in range(3):
        part = vec.astype(jnp.bfloat16).astype(jnp.float32)
        parts.append(part)
        vec = vec - part
    parts.append(jnp.zeros((LANES - 3 * blocks, slots), jnp.float32))
    split_ref[...] = jnp.concatenate(parts, axis=0).T.astype(jnp.bfloat16)


def column_scores(stream_ref, q, split_ref, blocks, k, lane_ref, p):
    lane = lax.broadcasted_iota(jnp.int32, (16, LANES), 1)
    pick = jnp.where((lane < 3 * blocks) & (lax.rem(lane, blocks) == k), 1.0, 0.0).astype(jnp.bfloat16)
    pick = jnp.concatenate([pick] * (split_ref.shape[0] // 16), axis=0)
    score = lax.dot_general(
        jnp.concatenate([whole_block(stream_ref, q), split_ref[...]], axis=1),
        jnp.concatenate([whole_block(lane_ref, p), pick], axis=1),
        (((1,), (1,)), ((), ())),
        preferred_element_type=jnp.float32,
    )
    return score, jnp.max(score, axis=0, keepdims=True)


def column_lse(*operands):
    score, peak = column_scores(*operands)
    return peak * UNIT, jnp.sum(jnp.exp2((score - peak) * UNIT), axis=0, keepdims=True)


def slots_of(tile, vec):
    found = vec[:, :LANES]
    for t in range(1, vec.shape[1] // LANES):
        found = jnp.where(tile == t, vec[:, t * LANES : (t + 1) * LANES], found)
    return found


def clear(peak_ref, sum_ref):
    peak_ref[...] = jnp.full(peak_ref.shape, FLOOR, jnp.float32)
    sum_ref[...] = jnp.zeros(sum_ref.shape, jnp.float32)


def merge_slots(peak, total, count):
    shape = (count, peak.shape[0] // count, peak.shape[1])
    peak = peak.reshape(shape)
    top = jnp.max(peak, axis=1, keepdims=True)
    total = jnp.sum(total.reshape(shape) * jnp.exp2(peak - top), axis=1)
    return top[:, 0] + jnp.log2(jnp.maximum(total, 1.0))


def pair_list(tb, list_ref, other_ref=None):
    own = list_ref[0]
    count = own if other_ref is None else own + other_ref[0]

    def pair(place):
        place = jnp.minimum(place, count - 1)
        if other_ref is None:
            code, shift = list_ref[1 + place], 0
        else:
            mine = place < own
            here, there = list_ref[1 + jnp.where(mine, place, 0)], other_ref[1 + jnp.where(mine, 0, place - own)]
            code = jnp.where(mine, here, there)
            shift = jnp.where(mine, 0, tb)
        return code // tb, lax.rem(code, tb) + shift

    return count, pair


def visit_pairs(pairs, first, last, group, work):
    count, pair = pairs

    @pl.loop(0, pl.cdiv(last - first, group))
    def _(step):
        places = [first + step * group + k for k in range(group)]
        work([pair(place) + (place < count,) for place in places])


def half_sweep(pairs, rows, x_ref, y_ref, tb, vec, scratch):
    split_ref, peak_ref, sum_ref = scratch
    sb = x_ref.shape[1]
    used = sb * tb
    split_columns(vec, split_ref)
    clear(peak_ref, sum_ref)

    def work(group):
        found = []
        for p, q, _ in group:
            if rows:
                found.append((p * tb + q, column_lse(y_ref, q, split_ref, tb, q, x_ref, p)))
            else:
                found.append((q * sb + p, column_lse(x_ref, p, split_ref, sb, p, y_ref, q)))
        for slot, pair in found:
            peak_ref[pl.ds(slot, 1), :], sum_ref[pl.ds(slot, 1), :] = pair

    count = pairs[0]
    rest = lax.rem(count, GROUP)
    large = jnp.where(rest > GROUP // 2, count, count - rest)
    middle = jnp.where(rest > GROUP // 4, count, large)
    visit_pairs(pairs, 0, large, GROUP, work)
    visit_pairs(pairs, large, middle, GROUP // 2, work)
    visit_pairs(pairs, middle, count, GROUP // 4, work)
    return merge_slots(peak_ref[:used], sum_ref[:used], sb if rows else tb)


def half_scratch(sb, tb, blk):
    return [
        pltpu.VMEM((blk, LANES), jnp.bfloat16),
        pltpu.VMEM((sb * tb, blk), jnp.float32),
        pltpu.VMEM((sb * tb, blk), jnp.float32),
    ]


def sweep_own(pairs, x_ref, y_ref, u, h, part_ref, scratch):
    sb, tb = u.shape[0], h.shape[0]
    part_ref[:sb] = half_sweep(pairs, True, x_ref, y_ref, tb, h, scratch)
    part_ref[sb:] = half_sweep(pairs, False, x_ref, y_ref, tb, u, scratch)


def sweep_shared(row_side, pairs, x_ref, y_ref, u, h, part_ref, scratch):
    sb, tb = u.shape[0], h.shape[0]
    odd = is_odd()
    summing_rows = odd if row_side else jnp.logical_not(odd)

    @pl.when(summing_rows)
    def _():
        part_ref[...] = padded(half_sweep(pairs, True, x_ref, y_ref, tb, h, scratch), part_ref)

    @pl.when(jnp.logical_not(summing_rows))
    def _():
        part_ref[...] = half_sweep(pairs, False, x_ref, y_ref, tb, u, scratch)


def project_scratch(sb, tb, blk, width):
    return [
        pltpu.VMEM((blk, LANES), jnp.bfloat16),
        pltpu.VMEM((tb, width, blk), jnp.bfloat16),
        pltpu.VMEM((sb + 1, 1, blk), jnp.float32),
        pltpu.VMEM((sb + 1, 1, blk), jnp.float32),
        pltpu.VMEM((sb + 1, width, blk), jnp.float32),
        pltpu.VMEM((sb, blk, width), jnp.float32),
    ]


def list_kernel(keep_ref, src_counts_ref, tgt_counts_ref, x_in_ref, y_in_ref, list_ref, x_ref, y_ref):
    sb, tb = keep_ref.shape
    x_ref[...] = x_in_ref[...]
    y_ref[...] = y_in_ref[...]
    counts_at = 1 + sb * tb
    n = jnp.int32(0)
    for code in range(sb * tb):
        list_ref[1 + n] = code
        n = n + (keep_ref[code // tb, code % tb] > 0).astype(jnp.int32)
    list_ref[0] = n
    for k in range(sb):
        list_ref[counts_at + k] = src_counts_ref[k]
    for k in range(tb):
        list_ref[counts_at + sb + k] = tgt_counts_ref[k]


def assemble(place, list_ref, counts_at, parts, part_refs, points_ref, vec_ref):
    n, blocks, piece, width = points_ref.shape
    blk = n * piece
    vec_ref[...] = jnp.zeros(vec_ref.shape, jnp.float32)
    for mask, first, k, count in parts:
        owner = jnp.bitwise_xor(place, mask)
        rows = min(count, blocks * piece - first)
        points_ref[owner, first // piece : (first + rows) // piece] = part_refs[k][:rows].reshape(
            rows // piece, piece, width
        )
        if rows < count:
            vecs = part_refs[k][rows:count].astype(jnp.float32)
            tile = owner * piece // LANES
            vec_ref[0, tile] += vecs[:blocks]
            vec_ref[1, tile] += vecs[blocks:]
    mass = jnp.concatenate([vec_ref[0, t] for t in range(blk // LANES)], axis=1)
    potential = jnp.concatenate([vec_ref[1, t] for t in range(blk // LANES)], axis=1) * UNIT
    block_of = lax.broadcasted_iota(jnp.int32, (blocks, blk), 0)
    slot_of = lax.broadcasted_iota(jnp.int32, (blocks, blk), 1)
    half = jnp.zeros((blocks, blk), jnp.float32)
    count = jnp.zeros((blocks, blk), jnp.int32)
    ones = jnp.ones((blocks, width), jnp.bfloat16)
    for k in range(blocks):
        wide = whole_block(points_ref, k).astype(jnp.float32)
        square = wide * wide
        high = square.astype(jnp.bfloat16)
        low = (square - high.astype(jnp.float32)).astype(jnp.bfloat16)
        norm = sum(
            lax.dot_general(ones, part, (((1,), (1,)), ((), ())), preferred_element_type=jnp.float32)
            for part in (high, low)
        )
        half = jnp.where(block_of == k, norm * (0.5 * UNIT), half)
        count = jnp.where(block_of == k, list_ref[counts_at + k], count)
    base = jnp.where(slot_of < count, jnp.log2(mass) - half, FLOOR)
    return potential, half, base


def first_kernel(x_parts, y_parts, list_ref, *refs):
    nx = 1 + max(part[2] for part in x_parts)
    ny = 1 + max(part[2] for part in y_parts)
    x_in, y_in, refs = refs[:nx], refs[nx : nx + ny], refs[nx + ny :]
    x_ref, y_ref, xfixed_ref, yfixed_ref, f_ref, part_ref, xvec_ref, yvec_ref = refs[:8]
    sb, tb = x_ref.shape[1], y_ref.shape[1]
    counts_at = 1 + sb * tb
    f, x_half, x_base = assemble(lax.axis_index("tgt"), list_ref, counts_at, x_parts, x_in, x_ref, xvec_ref)
    g, y_half, y_base = assemble(lax.axis_index("src"), list_ref, counts_at + sb, y_parts, y_in, y_ref, yvec_ref)
    f_ref[...] = f
    xfixed_ref[0], xfixed_ref[1] = x_half, x_base
    yfixed_ref[0], yfixed_ref[1], yfixed_ref[2] = y_half, y_base, g
    sweep_own(pair_list(tb, list_ref), x_ref, y_ref, f + x_base, g + y_base, part_ref, refs[8:])


def updated(old, half, lse):
    return 0.5 * (old + (half - lse))


def turned(cols):
    tb = cols.shape[0] // 2
    return jnp.concatenate([cols[tb:], cols[:tb]])


def second_kernel(list_ref, list2_ref, x_ref, y1_ref, y2_ref, xfixed_ref, yfixed1_ref, yfixed2_ref, f_in_ref, *refs):
    whole_ref, y_ref, yfixed_ref, mine_ref, part_ref = refs[:5]
    sb, tb = x_ref.shape[1], y1_ref.shape[1]
    y_ref[:, :tb] = y1_ref[...]
    y_ref[:, tb:] = y2_ref[...]
    half, base, g = [jnp.concatenate([yfixed1_ref[k], yfixed2_ref[k]]) for k in range(3)]
    yfixed_ref[0], yfixed_ref[1] = half, base
    f = updated(f_in_ref[...], xfixed_ref[0], whole_ref[:sb])
    g = updated(g, half, whole_ref[...])
    mine_ref[...] = jnp.where(is_odd(), padded(f, g), g)
    sweep_shared(
        0, pair_list(tb, list_ref, list2_ref), x_ref, y_ref, f + xfixed_ref[1], g + base, part_ref, refs[5:]
    )


def shared_kernel(row_side, list_ref, list2_ref, x_ref, y_ref, xfixed_ref, yfixed_ref, whole_ref, old_ref, *refs):
    mine_ref, part_ref = refs[:2]
    sb, tb = x_ref.shape[1], y_ref.shape[1] // 2
    f = updated(old_ref[:sb], xfixed_ref[0], whole_ref[:sb])
    g = updated(turned(old_ref[...]), yfixed_ref[0], whole_ref[...])
    mine_ref[...] = jnp.where(is_odd(), g, padded(f, g)) if row_side else jnp.where(is_odd(), padded(f, g), g)
    pairs = pair_list(tb, list_ref, list2_ref)
    sweep_shared(row_side, pairs, x_ref, y_ref, f + xfixed_ref[1], g + yfixed_ref[1], part_ref, refs[2:])


def step_kernel(list_ref, x_ref, y_ref, xfixed_ref, yfixed_in_ref, f_in_ref, whole_ref, *refs):
    yfixed_ref, f_ref, part_ref = refs[:3]
    sb, tb = x_ref.shape[1], y_ref.shape[1]
    f = updated(f_in_ref[...], xfixed_ref[0], whole_ref[:sb])
    half, base, g = [yfixed_in_ref[k] for k in range(3)]
    g = updated(g, half, whole_ref[sb:])
    f_ref[...] = f
    yfixed_ref[0], yfixed_ref[1], yfixed_ref[2] = half, base, g
    sweep_own(pair_list(tb, list_ref), x_ref, y_ref, f + xfixed_ref[1], g + base, part_ref, refs[3:])


def last_cols_kernel(row_side, list_ref, x_ref, y_ref, xfixed_ref, yfixed_in_ref, *refs):
    if row_side is None:
        f_in_ref, whole_ref, yfixed_ref, f_ref, cols_ref = refs[:5]
        scratch = refs[5:]
        sb, tb = x_ref.shape[1], cols_ref.shape[0]
        old_f, old_g = f_in_ref[...], yfixed_in_ref[2]
        rows, cols = whole_ref[:sb], whole_ref[sb:]
    else:
        whole_ref, whole2_ref, mine_ref, mine2_ref, yfixed_ref, f_ref, cols_ref = refs[:7]
        scratch = refs[7:]
        sb, tb = x_ref.shape[1], cols_ref.shape[0]
        has_rows = is_odd() if row_side else jnp.logical_not(is_odd())
        rows = jnp.where(has_rows, whole_ref[:sb], whole2_ref[:sb])
        cols = jnp.where(has_rows, whole2_ref[tb:], whole_ref[:tb])
        old_f = jnp.where(has_rows, mine2_ref[:sb], mine_ref[:sb])
        old_g = jnp.where(has_rows, mine_ref[:tb], mine2_ref[tb:])
    f = updated(old_f, xfixed_ref[0], rows)
    half, base = yfixed_in_ref[0, :tb], yfixed_in_ref[1, :tb]
    f_ref[...] = f
    yfixed_ref[0], yfixed_ref[1], yfixed_ref[2] = half, base, updated(old_g, half, cols)
    cols_ref[...] = half_sweep(pair_list(tb, list_ref), False, x_ref, y_ref, tb, f + xfixed_ref[1], scratch)


def last_rows_kernel(list_ref, x_ref, y_ref, yfixed_ref, rows_ref, *scratch):
    tb = yfixed_ref.shape[1]
    vec = yfixed_ref[2] + yfixed_ref[1]
    rows_ref[...] = half_sweep(pair_list(tb, list_ref), True, x_ref, y_ref, tb, vec, scratch)


def project_kernel(near, list_ref, x_ref, y_ref, yfixed_ref, rows_ref, *refs):
    col_refs, g_ref, out_refs = refs[:4], refs[4], refs[5 : 5 + near]
    split_ref, turned_ref, peak_ref, sum_ref, acc_ref, image_ref = refs[5 + near :]
    n, sb, piece, width = x_ref.shape
    tb = g_ref.shape[0]
    blk = n * piece
    g = updated(yfixed_ref[2], yfixed_ref[0], merge_lse([ref[...] for ref in col_refs]))
    g_ref[...] = g * (1.0 / UNIT)
    split_columns(g + yfixed_ref[1], split_ref)
    for q in range(tb):
        turned_ref[q] = whole_block(y_ref, q).T
    clear(peak_ref, sum_ref)
    acc_ref[...] = jnp.zeros(acc_ref.shape, jnp.float32)

    def move(group):
        found = []
        for p, q, real in group:
            score, peak = column_scores(y_ref, q, split_ref, tb, q, x_ref, p)
            weights = jnp.exp2((score - peak) * UNIT)
            high = weights.astype(jnp.bfloat16)
            low = (weights - high.astype(jnp.float32)).astype(jnp.bfloat16)
            ys = turned_ref[q]
            moved = jnp.dot(ys, high, preferred_element_type=jnp.float32) + jnp.dot(
                ys, low, preferred_element_type=jnp.float32
            )
            found.append((jnp.where(real, p, sb), peak * UNIT, jnp.sum(weights, axis=0, keepdims=True), moved))
        for p, peak, total, moved in found:
            old = peak_ref[p]
            new = jnp.maximum(old, peak)
            before, here = jnp.exp2(old - new), jnp.exp2(peak - new)
            peak_ref[p] = new
            sum_ref[p] = sum_ref[p] * before + total * here
            acc_ref[p] = acc_ref[p] * before + moved * here

    pairs = pair_list(tb, list_ref)
    rest = lax.rem(pairs[0], MOVE_GROUP)
    large = jnp.where(rest > MOVE_GROUP // 2, pairs[0], pairs[0] - rest)
    visit_pairs(pairs, 0, large, MOVE_GROUP, move)
    visit_pairs(pairs, large, pairs[0], MOVE_GROUP // 2, move)
    rows = []
    for p in range(sb):
        total = jnp.maximum(sum_ref[p], 1.0)
        image_ref[p] = (acc_ref[p] / total).T
        rows.append(peak_ref[p] + jnp.log2(total))
    lse = jnp.concatenate(rows, axis=0)

    me = lax.rem(lax.axis_index("tgt"), near)
    for e, out_ref in enumerate(out_refs):
        for far in range(4):
            owner = far * near + jnp.bitwise_xor(me, e)
            for p in range(sb):
                out_ref[far, p * piece : (p + 1) * piece] = image_ref[p, pl.ds(pl.multiple_of(owner * piece, piece), piece)]
            tile = owner * piece // LANES
            out_ref[far, sb * piece : sb * (piece + 1)] = slots_of(tile, lse)
            out_ref[far, sb * (piece + 1) :] = slots_of(tile, rows_ref[...])


def merge_images(parts, offset, sb, piece, turn_ref):
    whole = merge_lse([lse for _, lse in parts])
    weights = []
    for k, (_, lse) in enumerate(parts):
        turn_ref[k] = jnp.exp2(lse - whole).T
        weights.append(turn_ref[k, pl.ds(offset, piece), :])
    images = []
    for p in range(sb):
        images.append(
            sum(
                image[p * piece : (p + 1) * piece] * weight[:, p : p + 1]
                for (image, _), weight in zip(parts, weights)
            )
        )
    return images, whole


def near_kernel(near, sb, piece, *refs):
    in_refs, out_refs, turn_ref = refs[:near], refs[near : near + 4], refs[near + 4]
    place = lax.axis_index("tgt")
    me, mine = lax.rem(place, near), place // near
    rows = sb * piece
    for d, out_ref in enumerate(out_refs):
        far = jnp.bitwise_xor(mine, d)
        offset = lax.rem((far * near + me) * piece, LANES)
        parts = [(ref[far, :rows], ref[far, rows : rows + sb]) for ref in in_refs]
        images, whole = merge_images(parts, pl.multiple_of(offset, piece), sb, piece, turn_ref)
        for p in range(sb):
            out_ref[p * piece : (p + 1) * piece] = images[p]
        out_ref[rows : rows + sb] = whole
        out_ref[rows + sb :] = merge_lse([ref[far, rows + sb :] for ref in in_refs])


def far_kernel(sb, piece, xfixed_ref, f_in_ref, *refs):
    in_refs, out_ref, f_ref, turn_ref = refs[:4], refs[4], refs[5], refs[6]
    rows = sb * piece
    start = lax.axis_index("tgt") * piece
    offset = lax.rem(start, LANES)
    parts = [(ref[:rows], ref[rows : rows + sb]) for ref in in_refs]
    images, _ = merge_images(parts, pl.multiple_of(offset, piece), sb, piece, turn_ref)
    for p in range(sb):
        out_ref[p] = images[p]
    tile = start // LANES
    lse = merge_lse([ref[rows + sb :] for ref in in_refs])
    f = updated(slots_of(tile, f_in_ref[...]), slots_of(tile, xfixed_ref[0]), lse)
    f_ref[...] = pltpu.roll(f * (1.0 / UNIT), lax.rem(LANES - offset, LANES), 1)[:, :piece]


def pack_kernel(*refs):
    for k, axis in enumerate(("tgt", "src")):
        points_ref, mass_ref, potential_ref = refs[3 * k : 3 * k + 3]
        out_ref = refs[6 + k]
        blocks, piece, width = points_ref.shape
        here = lax.rem(lax.axis_index(axis) * piece, LANES)
        slot = lax.broadcasted_iota(jnp.int32, (piece, LANES), 0)
        lane = lax.broadcasted_iota(jnp.int32, (piece, LANES), 1)
        put = jnp.where(lane == slot + here, 1.0, 0.0).astype(jnp.bfloat16)
        vecs = [jnp.dot(ref[...], put, preferred_element_type=jnp.float32) for ref in (mass_ref, potential_ref)]
        out_ref[: blocks * piece] = points_ref[...].reshape(blocks * piece, width)
        out_ref[blocks * piece :] = jnp.concatenate(vecs, axis=0).astype(jnp.bfloat16)


def on_device(
    src_points, tgt_points, src_mass, tgt_mass, src_potential, tgt_potential, src_counts, tgt_counts, keep
):
    ntgt, nsrc = lax.axis_size("tgt"), lax.axis_size("src")
    near = near_count("tgt")
    sb, src_piece, width = src_points.shape
    tb, tgt_piece, _ = tgt_points.shape
    blk = src_piece * ntgt
    x_rows, y_rows = sb * src_piece, tb * tgt_piece
    x_packed, y_packed = pl.pallas_call(
        pack_kernel,
        out_shape=(
            jax.ShapeDtypeStruct((x_rows + 2 * sb, width), jnp.bfloat16),
            jax.ShapeDtypeStruct((y_rows + 2 * tb, width), jnp.bfloat16),
        ),
        in_specs=[VMEM] * 6,
        out_specs=(VMEM, VMEM),
        name="pack",
    )(src_points, src_mass, src_potential, tgt_points, tgt_mass, tgt_potential)
    (x_in, x_parts), (y_in, y_parts) = gather_points(x_packed, y_packed, y_rows)
    pairs, x_own, y_own = pl.pallas_call(
        list_kernel,
        out_shape=(
            jax.ShapeDtypeStruct((1 + sb * tb + sb + tb,), jnp.int32),
            jax.ShapeDtypeStruct(x_packed.shape, x_packed.dtype),
            jax.ShapeDtypeStruct(y_packed.shape, y_packed.dtype),
        ),
        in_specs=[SMEM] * 3 + [VMEM] * 2,
        out_specs=(SMEM, VMEM, VMEM),
        compiler_params=PARAMS,
        name="kept_pairs",
    )(keep, src_counts, tgt_counts, x_packed, y_packed)
    x_in[0], y_in[0] = x_own, y_own

    def half_room(targets):
        return dict(scratch_shapes=half_scratch(sb, targets, blk), compiler_params=PARAMS)

    shared = shared_rows()
    x, y, xfixed, yfixed, f, part = pl.pallas_call(
        functools.partial(first_kernel, x_parts, y_parts),
        out_shape=(
            jax.ShapeDtypeStruct((ntgt, sb, src_piece, width), jnp.bfloat16),
            jax.ShapeDtypeStruct((nsrc, tb, tgt_piece, width), jnp.bfloat16),
            f32(2, sb, blk),
            f32(3, tb, blk),
            f32(sb, blk),
            f32(sb + tb, blk),
        ),
        in_specs=[SMEM] + [VMEM] * (len(x_in) + len(y_in)),
        out_specs=(VMEM,) * 6,
        scratch_shapes=[
            pltpu.VMEM((2, blk // LANES, sb, LANES), jnp.float32),
            pltpu.VMEM((2, blk // LANES, tb, LANES), jnp.float32),
        ]
        + half_scratch(sb, tb, blk),
        compiler_params=PARAMS,
        name="first_sweep",
    )(pairs, *x_in, *y_in)

    if shared:
        pairs_two, y_two, yfixed_two = [swap(array, "tgt", 1) for array in (pairs, y, yfixed)]
        pairs_two, part = lax.optimization_barrier((pairs_two, part))
        whole = exchange_first(part, sb)
        y, yfixed, mine, part = pl.pallas_call(
            second_kernel,
            out_shape=(
                jax.ShapeDtypeStruct((nsrc, 2 * tb, tgt_piece, width), jnp.bfloat16),
                f32(2, 2 * tb, blk),
                f32(2 * tb, blk),
                f32(2 * tb, blk),
            ),
            in_specs=[SMEM] * 2 + [VMEM] * 8,
            out_specs=(VMEM,) * 4,
            name="second_sweep",
            **half_room(2 * tb),
        )(pairs, pairs_two, x, y, y_two, xfixed, yfixed, yfixed_two, f, whole)
        for k in range(2, ITERS - 1):
            old, whole = swap(mine, "tgt", 1), exchange_shared(part, (k - 1) % 2 ^ 1)
            mine, part = pl.pallas_call(
                functools.partial(shared_kernel, k % 2 ^ 1),
                out_shape=(f32(2 * tb, blk), f32(2 * tb, blk)),
                in_specs=[SMEM] * 2 + [VMEM] * 6,
                out_specs=(VMEM, VMEM),
                name="sweep",
                **half_room(2 * tb),
            )(pairs, pairs_two, x, y, xfixed, yfixed, whole, old)
        row_side = (ITERS - 2) % 2 ^ 1
        old, whole = swap(mine, "tgt", 1), exchange_shared(part, row_side)
        last = (whole, swap(whole, "tgt", 1), mine, old)
    else:
        step = pl.pallas_call(
            step_kernel,
            out_shape=(f32(3, tb, blk), f32(sb, blk), f32(sb + tb, blk)),
            in_specs=[SMEM] + [VMEM] * 6,
            out_specs=(VMEM,) * 3,
            name="sweep",
            **half_room(tb),
        )
        for _ in range(ITERS - 2):
            yfixed, f, part = step(pairs, x, y, xfixed, yfixed, f, exchange_plain(part, sb))
        row_side, last = None, (f, exchange_plain(part, sb))

    yfixed, f, cols = pl.pallas_call(
        functools.partial(last_cols_kernel, row_side),
        out_shape=(f32(3, tb, blk), f32(sb, blk), f32(tb, blk)),
        in_specs=[SMEM] + [VMEM] * (4 + len(last)),
        out_specs=(VMEM,) * 3,
        name="last_cols",
        **half_room(tb),
    )(pairs, x, y, xfixed, yfixed, *last)
    col_parts = exchange_lse(cols, "src")
    rows = pl.pallas_call(
        last_rows_kernel,
        out_shape=f32(sb, blk),
        in_specs=[SMEM] + [VMEM] * 3,
        out_specs=VMEM,
        name="last_rows",
        **half_room(tb),
    )(pairs, x, y, yfixed)
    rows, *col_parts = lax.optimization_barrier((rows, *col_parts))
    tile = sb * (src_piece + 2)
    g, *near_parts = pl.pallas_call(
        functools.partial(project_kernel, near),
        out_shape=(f32(tb, blk),) + (f32(4, tile, width),) * near,
        in_specs=[SMEM] + [VMEM] * 8,
        out_specs=(VMEM,) * (1 + near),
        scratch_shapes=project_scratch(sb, tb, blk, width),
        compiler_params=PARAMS,
        name="project",
    )(pairs, x, y, yfixed, rows, *col_parts)
    if near > 1:
        near_parts = near_parts[:1] + [swap(near_parts[d], "tgt", d) for d in range(1, near)]
    far_parts = pl.pallas_call(
        functools.partial(near_kernel, near, sb, src_piece),
        out_shape=(f32(tile, width),) * 4,
        in_specs=[VMEM] * near,
        out_specs=(VMEM,) * 4,
        scratch_shapes=[pltpu.VMEM((near, LANES, sb), jnp.float32)],
        compiler_params=PARAMS,
        name="merge_near",
    )(*near_parts)
    far_parts = [far_parts[0]] + [swap(far_parts[k], "tgt", near * k) for k in range(1, 4)]
    images, src_final = pl.pallas_call(
        functools.partial(far_kernel, sb, src_piece),
        out_shape=(f32(sb, src_piece, width), f32(sb, src_piece)),
        in_specs=[VMEM] * 6,
        out_specs=(VMEM, VMEM),
        scratch_shapes=[pltpu.VMEM((4, LANES, sb), jnp.float32)],
        compiler_params=PARAMS,
        name="merge_far",
    )(xfixed, f, *far_parts)

    tgt_final = lax.dynamic_slice_in_dim(g, lax.axis_index("src") * tgt_piece, tgt_piece, 1)
    return images, src_final, tgt_final


def solution(mesh):
    return jax.shard_map(
        on_device,
        mesh=mesh,
        in_specs=(
            P("src", "tgt", None),
            P("tgt", "src", None),
            P("src", "tgt"),
            P("tgt", "src"),
            P("src", "tgt"),
            P("tgt", "src"),
            P("src"),
            P("tgt"),
            P("src", "tgt"),
        ),
        out_specs=(P("src", "tgt", None), P("src", "tgt"), P("tgt", "src")),
        check_vma=False,
    )
```

profile of v0, /device:TPU:0, one launch (start us, length us, event | category | flops | bytes accessed | tf_op | source)
XLA Modules:
  0.0 84.8 jit_solution(5263308456655407524)
XLA Ops:
  0.6 1.7 %pack.1 = (bf16[272,128]{1,0:T(8,128)(2,1)}, bf16[528,128]{1,0:T(8,128)(2,1)}) custom-call(bf16[8,32,128]{2,1,0:T(8,128)(2,1)} %refs_0_.1, bf16[8,32]{1,0:T(8,128)(2,1)} %refs_1_.1, bf16[8,32]{1,0:T(8,128)(2,1)} %refs_2_.1, bf16[8,64,128]{2,1,0:T(8,128)(2,1)} %refs_3_.1, bf16[8,64]{1,0:T(8,128)(2,1)} %refs_4_.1, bf16[8,64]{1,0:T(8,128)(2,1)} %refs_5_.1), custom_call_target="tpu_custom_call" | custom-call | tf_op jit(solution)/shard_map/pack/pallas_call | solution.py:525
  2.4 5.1 %collective-permute-start.1 = (bf16[528,128]{1,0:T(8,128)(2,1)}, bf16[528,128]{1,0:T(8,128)(2,1)S(1)}, u32[]{:S(2)}, u32[]{:S(2)}) collective-permute-start(bf16[528,128]{1,0:T(8,128)(2,1)} %get-tuple-element.45.y_in_ref), channel_id=1, source_target_pairs={{0,24},{8,16},{16,8},{24,0},{1,25},{9,17},{17,9},{25,1},{2,26},{10... | collective-permute-start | bytes 405512 | tf_op jit(solution)/shard_map/ppermute | solution.py:30
  7.5 2.4 %collective-permute-start.4 = (bf16[272,128]{1,0:T(8,128)(2,1)}, bf16[272,128]{1,0:T(8,128)(2,1)S(1)}, u32[]{:S(2)}, u32[]{:S(2)}) collective-permute-start(bf16[272,128]{1,0:T(8,128)(2,1)} %get-tuple-element.44.x_in_ref), channel_id=1, source_target_pairs={{0,6},{1,7},{2,4},{3,5},{4,2},{5,3},{6,0},{7,1},{8,14},{9,15},{10,... | collective-permute-start | bytes 208904 | tf_op jit(solution)/shard_map/ppermute | solution.py:30
  11.0 2.0 %collective-permute-done.4.refs_3_ = bf16[272,128]{1,0:T(8,128)(2,1)S(1)} collective-permute-done((bf16[272,128]{1,0:T(8,128)(2,1)}, bf16[272,128]{1,0:T(8,128)(2,1)S(1)}, u32[]{:S(2)}, u32[]{:S(2)}) %collective-permute-start.4) | collective-permute-done | bytes 69664 | tf_op jit(solution)/shard_map/ppermute | solution.py:30
  19.2 1.9 %collective-permute-done.9.refs_10_ = bf16[528,128]{1,0:T(8,128)(2,1)S(1)} collective-permute-done((bf16[528,128]{1,0:T(8,128)(2,1)}, bf16[528,128]{1,0:T(8,128)(2,1)S(1)}, u32[]{:S(2)}, u32[]{:S(2)}) %collective-permute-start.9) | collective-permute-done | bytes 135200 | tf_op jit(solution)/shard_map/ppermute | solution.py:30
  21.1 5.1 %first_sweep.1 = (bf16[8,8,32,128]{3,2,1,0:T(8,128)(2,1)S(1)}, bf16[4,8,64,128]{3,2,1,0:T(8,128)(2,1)S(1)}, f32[2,8,256]{2,1,0:T(8,128)S(1)}, f32[3,8,256]{2,1,0...) custom-call(s32[81]{0:T(128)S(1)} %get-tuple-element.46.list_ref, ...), custom_call_target="tpu_custom_call" | custom-call | tf_op jit(solution)/shard_map/first_sweep/pallas_call | solution.py:554
  29.2 1.9 %collective-permute-start.14 = (f32[16,256]{1,0:T(8,128)S(1)}, f32[16,256]{1,0:T(8,128)S(1)}, u32[]{:S(2)}, u32[]{:S(2)}) collective-permute-start(f32[16,256]{1,0:T(8,128)S(1)} %maximum_select_fusion), channel_id=1, source_target_pairs={{0,8},{1,3},{2,10},{3,1},{4,12},{5,7},{6,14},{7,5},{8,0},{9,11},{1... | collective-permute-start | bytes 49160 | tf_op jit(solution)/shard_map/ppermute | solution.py:81
  33.2 3.6 %second_sweep.1 = (bf16[4,16,64,128]{3,2,1,0:T(8,128)(2,1)S(1)}, f32[2,16,256]{2,1,0:T(8,128)S(1)}, f32[16,256]{1,0:T(8,128)S(1)}, f32[16,256]{1,0:T(8,128)S(1)}) custom-call(s32[81]{0:T(128)S(1)} %get-tuple-element.46.list_ref, s32[81]{0:T(128)S(1)} %collective-permute-done.10.list2_ref, bf16[8,8,32,128]{3,2,1,0:T(8,128)(2,1)S(1)} %get-tuple-element.55.x_ref, ...), custom_call_target="tpu_custom_call" | custom-call | tf_op jit(solution)/shard_map/second_sweep/pallas_call | solution.py:579
  36.8 3.2 %collective-permute-start.19 = (f32[16,256]{1,0:T(8,128)S(1)}, f32[16,256]{1,0:T(8,128)S(1)}, u32[]{:S(2)}, u32[]{:S(2)}) collective-permute-start(f32[16,256]{1,0:T(8,128)S(1)} %get-tuple-element.64), channel_id=1, source_target_pairs={{0,6},{1,17},{2,4},{3,19},{4,2},{5,21},{6,0},{7,23},{8,14},{9,25},... | collective-permute-start | bytes 49160 | tf_op jit(solution)/shard_map/ppermute | solution.py:81
  40.0 1.9 %collective-permute-start.18 = (f32[16,256]{1,0:T(8,128)S(1)}, f32[16,256]{1,0:T(8,128)S(1)}, u32[]{:S(2)}, u32[]{:S(2)}) collective-permute-start(f32[16,256]{1,0:T(8,128)S(1)} %get-tuple-element.64), channel_id=1, source_target_pairs={{0,4},{1,25},{2,6},{3,27},{4,0},{5,29},{6,2},{7,31},{8,12},{9,17},... | collective-permute-start | bytes 49160 | tf_op jit(solution)/shard_map/ppermute | solution.py:81
  41.9 1.9 %collective-permute-done.18 = f32[16,256]{1,0:T(8,128)S(1)} collective-permute-done((f32[16,256]{1,0:T(8,128)S(1)}, f32[16,256]{1,0:T(8,128)S(1)}, u32[]{:S(2)}, u32[]{:S(2)}) %collective-permute-start.18) | collective-permute-done | bytes 16416 | tf_op jit(solution)/shard_map/ppermute | solution.py:81
  43.7 1.9 %collective-permute-done.17 = f32[16,256]{1,0:T(8,128)S(1)} collective-permute-done((f32[16,256]{1,0:T(8,128)S(1)}, f32[16,256]{1,0:T(8,128)S(1)}, u32[]{:S(2)}, u32[]{:S(2)}) %collective-permute-start.17) | collective-permute-done | bytes 16416 | tf_op jit(solution)/shard_map/ppermute | solution.py:81
  45.6 3.3 %sweep.1 = (f32[16,256]{1,0:T(8,128)S(1)}, f32[16,256]{1,0:T(8,128)S(1)}) custom-call(s32[81]{0:T(128)S(1)} %get-tuple-element.46.list_ref, s32[81]{0:T(128)S(1)} %collective-permute-done.10.list2_ref, bf16[8,8,32,128]{3,2,1,0:T(8,128)(2,1)S(1)} %get-tuple-element.55.x_ref, bf16[4,16,64,128]{3,2,1,0:T(8,128)(2,1)S(1)} %get-tuple-element.62.y_ref, ...), custom_call_target="tpu_custom_call" | custom-call | tf_op jit(solution)/shard_map/sweep/pallas_call | solution.py:594
  50.6 2.0 %collective-permute-start.21 = (f32[16,256]{1,0:T(8,128)S(1)}, f32[16,256]{1,0:T(8,128)S(1)}, u32[]{:S(2)}, u32[]{:S(2)}) collective-permute-start(f32[16,256]{1,0:T(8,128)S(1)} %get-tuple-element.66), channel_id=1, source_target_pairs={{0,8},{1,3},{2,10},{3,1},{4,12},{5,7},{6,14},{7,5},{8,0},{9,11},{1... | collective-permute-start | bytes 49160 | tf_op jit(solution)/shard_map/ppermute | solution.py:81
  53.7 1.6 %collective-permute-done.22 = f32[16,256]{1,0:T(8,128)S(1)} collective-permute-done((f32[16,256]{1,0:T(8,128)S(1)}, f32[16,256]{1,0:T(8,128)S(1)}, u32[]{:S(2)}, u32[]{:S(2)}) %collective-permute-start.22) | collective-permute-done | bytes 16416 | tf_op jit(solution)/shard_map/ppermute | solution.py:81
  56.6 2.5 %last_cols.1 = (f32[3,8,256]{2,1,0:T(8,128)S(1)}, f32[8,256]{1,0:T(8,128)S(1)}, f32[8,256]{1,0:T(8,128)S(1)}) custom-call(s32[81]{0:T(128)S(1)} %get-tuple-element.46.list_ref, bf16[8,8,32,128]{3,2,1,0:T(8,128)(2,1)S(1)} %get-tuple-element.55.x_ref, bf16[4,16,64,128]{3,2,1,0:T(8,128)(2,1)S(1)} %get-tuple-element.62.y_ref, ...), custom_call_target="tpu_custom_call" | custom-call | tf_op jit(solution)/shard_map/last_cols/pallas_call | solution.py:618
  59.1 2.1 %collective-permute-start.28 = (f32[8,256]{1,0:T(8,128)S(1)}, f32[8,256]{1,0:T(8,128)S(1)}, u32[]{:S(2)}, u32[]{:S(2)}) collective-permute-start(f32[8,256]{1,0:T(8,128)S(1)} %get-tuple-element.72.refs_0_), channel_id=1, source_target_pairs={{0,24},{8,16},{16,8},{24,0},{1,25},{9,17},{17,9},{25,1},{2,26},{10... | collective-permute-start | bytes 24584 | tf_op jit(solution)/shard_map/ppermute | solution.py:30
  61.2 2.4 %collective-permute-start.26 = (f32[8,256]{1,0:T(8,128)S(1)}, f32[8,256]{1,0:T(8,128)S(1)}, u32[]{:S(2)}, u32[]{:S(2)}) collective-permute-start(f32[8,256]{1,0:T(8,128)S(1)} %get-tuple-element.72.refs_0_), channel_id=1, source_target_pairs={{0,8},{8,0},{16,24},{24,16},{1,9},{9,1},{17,25},{25,17},{2,10},{10... | collective-permute-start | bytes 24584 | tf_op jit(solution)/shard_map/ppermute | solution.py:30
  63.5 2.5 %last_rows.1.rows_ref = f32[8,256]{1,0:T(8,128)S(1)} custom-call(s32[81]{0:T(128)S(1)} %get-tuple-element.46.list_ref, bf16[8,8,32,128]{3,2,1,0:T(8,128)(2,1)S(1)} %get-tuple-element.55.x_ref, bf16[4,16,64,128]{3,2,1,0:T(8,128)(2,1)S(1)} %get-tuple-element.62.y_ref, f32[3,8,256]{2,1,0:T(8,128)S(1)} %get-tuple-element.69.yfixed_ref), custom_call_target="tpu_custom_call" | custom-call | tf_op jit(solution)/shard_map/last_rows/pallas_call | solution.py:627
  66.1 4.3 %project.1 = (f32[8,256]{1,0:T(8,128)S(1)}, f32[4,272,128]{2,1,0:T(8,128)S(1)}, f32[4,272,128]{2,1,0:T(8,128)S(1)}) custom-call(s32[81]{0:T(128)S(1)} %get-tuple-element.46.list_ref, bf16[8,8,32,128]{3,2,1,0:T(8,128)(2,1)S(1)} %get-tuple-element.55.x_ref, bf16[4,16,64,128]{3,2,1,0:T(8,128)(2,1)S(1)} %get-tuple-element.62.y_ref, ...), custom_call_target="tpu_custom_call" | custom-call | tf_op jit(solution)/shard_map/project/pallas_call | solution.py:637
  70.5 1.9 %collective-permute-done.29.refs_1_ = f32[4,272,128]{2,1,0:T(8,128)S(1)} collective-permute-done((f32[4,272,128]{2,1,0:T(8,128)S(1)}, f32[4,272,128]{2,1,0:T(8,128)S(1)}, u32[]{:S(2)}, u32[]{:S(2)}) %collective-permute-start.29) | collective-permute-done | bytes 557088 | tf_op jit(solution)/shard_map/ppermute | solution.py:30
  73.1 2.2 %collective-permute-start.30 = (f32[272,128]{1,0:T(8,128)S(1)}, f32[272,128]{1,0:T(8,128)S(1)}, u32[]{:S(2)}, u32[]{:S(2)}) collective-permute-start(f32[272,128]{1,0:T(8,128)S(1)} %get-tuple-element.79), channel_id=1, source_target_pairs={{0,2},{1,3},{2,0},{3,1},{4,6},{5,7},{6,4},{7,5},{8,10},{9,11},{10,... | collective-permute-start | bytes 417800 | tf_op jit(solution)/shard_map/ppermute | solution.py:30
  77.5 2.0 %collective-permute-done.30.refs_1_ = f32[272,128]{1,0:T(8,128)S(1)} collective-permute-done((f32[272,128]{1,0:T(8,128)S(1)}, f32[272,128]{1,0:T(8,128)S(1)}, u32[]{:S(2)}, u32[]{:S(2)}) %collective-permute-start.30) | collective-permute-done | bytes 139296 | tf_op jit(solution)/shard_map/ppermute | solution.py:30
  79.5 4.2 %collective-permute-done.31.refs_2_ = f32[272,128]{1,0:T(8,128)S(1)} collective-permute-done((f32[272,128]{1,0:T(8,128)S(1)}, f32[272,128]{1,0:T(8,128)S(1)}, u32[]{:S(2)}, u32[]{:S(2)}) %collective-permute-start.31) | collective-permute-done | bytes 139296 | tf_op jit(solution)/shard_map/ppermute | solution.py:30
  (68 shorter events, 20.4 us)
Async XLA Ops:
  2.4 12.6 %collective-permute-start.1 = (bf16[528,128]{1,0:T(8,128)(2,1)}, bf16[528,128]{1,0:T(8,128)(2,1)S(1)}, u32[]{:S(2)}, u32[]{:S(2)}) collective-permute-start(bf16[528,128]{1,0:T(8,128)(2,1)} %get-tuple-element.45.y_in_ref), channel_id=1, source_target_pairs={{0,24},{8,16},{16,8},{24,0},{1,25},{9,17},{17,9},{25,1},{2,26},{10... | collective-permute-start | bytes 405512 | tf_op jit(solution)/shard_map/ppermute | solution.py:30
  7.5 7.5 %collective-permute-start = (bf16[528,128]{1,0:T(8,128)(2,1)}, bf16[528,128]{1,0:T(8,128)(2,1)S(1)}, u32[]{:S(2)}, u32[]{:S(2)}) collective-permute-start(bf16[528,128]{1,0:T(8,128)(2,1)} %get-tuple-element.45.y_in_ref), channel_id=1, source_target_pairs={{0,8},{8,0},{16,24},{24,16},{1,9},{9,1},{17,25},{25,17},{2,10},{10... | collective-permute-start | bytes 405512 | tf_op jit(solution)/shard_map/ppermute | solution.py:30
  7.5 5.5 %collective-permute-start.4 = (bf16[272,128]{1,0:T(8,128)(2,1)}, bf16[272,128]{1,0:T(8,128)(2,1)S(1)}, u32[]{:S(2)}, u32[]{:S(2)}) collective-permute-start(bf16[272,128]{1,0:T(8,128)(2,1)} %get-tuple-element.44.x_in_ref), channel_id=1, source_target_pairs={{0,6},{1,7},{2,4},{3,5},{4,2},{5,3},{6,0},{7,1},{8,14},{9,15},{10,... | collective-permute-start | bytes 208904 | tf_op jit(solution)/shard_map/ppermute | solution.py:30
  9.9 4.5 %collective-permute-start.3 = (bf16[272,128]{1,0:T(8,128)(2,1)}, bf16[272,128]{1,0:T(8,128)(2,1)S(1)}, u32[]{:S(2)}, u32[]{:S(2)}) collective-permute-start(bf16[272,128]{1,0:T(8,128)(2,1)} %get-tuple-element.44.x_in_ref), channel_id=1, source_target_pairs={{0,4},{1,5},{2,6},{3,7},{4,0},{5,1},{6,2},{7,3},{8,12},{9,13},{10,... | collective-permute-start | bytes 208904 | tf_op jit(solution)/shard_map/ppermute | solution.py:30
  10.4 4.5 %collective-permute-start.2 = (bf16[272,128]{1,0:T(8,128)(2,1)}, bf16[272,128]{1,0:T(8,128)(2,1)S(1)}, u32[]{:S(2)}, u32[]{:S(2)}) collective-permute-start(bf16[272,128]{1,0:T(8,128)(2,1)} %get-tuple-element.44.x_in_ref), channel_id=1, source_target_pairs={{0,2},{1,3},{2,0},{3,1},{4,6},{5,7},{6,4},{7,5},{8,10},{9,11},{10,... | collective-permute-start | bytes 208904 | tf_op jit(solution)/shard_map/ppermute | solution.py:30
  13.0 8.1 %collective-permute-start.9 = (bf16[528,128]{1,0:T(8,128)(2,1)}, bf16[528,128]{1,0:T(8,128)(2,1)S(1)}, u32[]{:S(2)}, u32[]{:S(2)}) collective-permute-start(bf16[528,128]{1,0:T(8,128)(2,1)} %get-tuple-element.45.y_in_ref), channel_id=1, source_target_pairs={{0,16},{8,24},{16,0},{24,8},{1,17},{9,25},{17,1},{25,9},{2,18},{10... | collective-permute-start | bytes 405512 | tf_op jit(solution)/shard_map/ppermute | solution.py:30
  14.4 4.3 %collective-permute-start.5 = (bf16[272,128]{1,0:T(8,128)(2,1)}, bf16[272,128]{1,0:T(8,128)(2,1)S(1)}, u32[]{:S(2)}, u32[]{:S(2)}) collective-permute-start(bf16[272,128]{1,0:T(8,128)(2,1)} %get-tuple-element.44.x_in_ref), channel_id=1, source_target_pairs={{0,1},{1,0},{2,3},{3,2},{4,5},{5,4},{6,7},{7,6},{8,9},{9,8},{10,11... | collective-permute-start | bytes 208904 | tf_op jit(solution)/shard_map/ppermute | solution.py:30
  15.0 6.1 %collective-permute-start.6 = (bf16[272,128]{1,0:T(8,128)(2,1)S(1)}, bf16[272,128]{1,0:T(8,128)(2,1)S(1)}, u32[]{:S(2)}, u32[]{:S(2)}) collective-permute-start(bf16[272,128]{1,0:T(8,128)(2,1)S(1)} %collective-permute-done.2.refs_1_), channel_id=1, source_target_pairs={{0,1},{1,0},{2,3},{3,2},{4,5},{5,4},{6,7},{7,6},{8,9},{9,8},{10,11... | collective-permute-start | bytes 208904 | tf_op jit(solution)/shard_map/ppermute | solution.py:30
  15.0 6.1 %collective-permute-start.7 = (bf16[272,128]{1,0:T(8,128)(2,1)S(1)}, bf16[272,128]{1,0:T(8,128)(2,1)S(1)}, u32[]{:S(2)}, u32[]{:S(2)}) collective-permute-start(bf16[272,128]{1,0:T(8,128)(2,1)S(1)} %collective-permute-done.3.refs_2_), channel_id=1, source_target_pairs={{0,1},{1,0},{2,3},{3,2},{4,5},{5,4},{6,7},{7,6},{8,9},{9,8},{10,11... | collective-permute-start | bytes 208904 | tf_op jit(solution)/shard_map/ppermute | solution.py:30
  15.5 5.6 %collective-permute-start.8 = (bf16[272,128]{1,0:T(8,128)(2,1)S(1)}, bf16[272,128]{1,0:T(8,128)(2,1)S(1)}, u32[]{:S(2)}, u32[]{:S(2)}) collective-permute-start(bf16[272,128]{1,0:T(8,128)(2,1)S(1)} %collective-permute-done.4.refs_3_), channel_id=1, source_target_pairs={{0,1},{1,0},{2,3},{3,2},{4,5},{5,4},{6,7},{7,6},{8,9},{9,8},{10,11... | collective-permute-start | bytes 208904 | tf_op jit(solution)/shard_map/ppermute | solution.py:30
  18.7 7.5 %collective-permute-start.10 = (s32[81]{0:T(128)S(1)}, s32[81]{0:T(128)S(1)}, u32[]{:S(2)}, u32[]{:S(2)}) collective-permute-start(s32[81]{0:T(128)S(1)} %get-tuple-element.46.list_ref), channel_id=1, source_target_pairs={{0,1},{1,0},{2,3},{3,2},{4,5},{5,4},{6,7},{7,6},{8,9},{9,8},{10,11... | collective-permute-start | bytes 980 | tf_op jit(solution)/shard_map/ppermute | solution.py:30
  26.3 6.9 %collective-permute-start.11 = (bf16[4,8,64,128]{3,2,1,0:T(8,128)(2,1)S(1)}, bf16[4,8,64,128]{3,2,1,0:T(8,128)(2,1)S(1)}, u32[]{:S(2)}, u32[]{:S(2)}) collective-permute-start(bf16[4,8,64,128]{3,2,1,0:T(8,128)(2,1)S(1)} %get-tuple-element.58.y1_ref), channel_id=1, source_target_pairs={{0,1},{1,0},{2,3},{3,2},{4,5},{5,4},{6,7},{7,6},{8,9},{9,8},{10,11... | collective-permute-start | bytes 1572872 | tf_op jit(solution)/shard_map/ppermute | solution.py:30
  27.5 4.7 %collective-permute-start.16 = (f32[16,256]{1,0:T(8,128)S(1)}, f32[16,256]{1,0:T(8,128)S(1)}, u32[]{:S(2)}, u32[]{:S(2)}) collective-permute-start(f32[16,256]{1,0:T(8,128)S(1)} %maximum_select_fusion), channel_id=1, source_target_pairs={{0,16},{1,7},{2,18},{3,5},{4,20},{5,3},{6,22},{7,1},{8,24},{9,15},... | collective-permute-start | bytes 49160 | tf_op jit(solution)/shard_map/ppermute | solution.py:81
  27.6 5.6 %collective-permute-start.15 = (f32[16,256]{1,0:T(8,128)S(1)}, f32[16,256]{1,0:T(8,128)S(1)}, u32[]{:S(2)}, u32[]{:S(2)}) collective-permute-start(f32[16,256]{1,0:T(8,128)S(1)} %maximum_select_fusion), channel_id=1, source_target_pairs={{0,24},{1,5},{2,26},{3,7},{4,28},{5,1},{6,30},{7,3},{8,16},{9,13},... | collective-permute-start | bytes 49160 | tf_op jit(solution)/shard_map/ppermute | solution.py:81
  36.8 5.0 %collective-permute-start.19 = (f32[16,256]{1,0:T(8,128)S(1)}, f32[16,256]{1,0:T(8,128)S(1)}, u32[]{:S(2)}, u32[]{:S(2)}) collective-permute-start(f32[16,256]{1,0:T(8,128)S(1)} %get-tuple-element.64), channel_id=1, source_target_pairs={{0,6},{1,17},{2,4},{3,19},{4,2},{5,21},{6,0},{7,23},{8,14},{9,25},... | collective-permute-start | bytes 49160 | tf_op jit(solution)/shard_map/ppermute | solution.py:81
  49.0 4.7 %collective-permute-start.23 = (f32[16,256]{1,0:T(8,128)S(1)}, f32[16,256]{1,0:T(8,128)S(1)}, u32[]{:S(2)}, u32[]{:S(2)}) collective-permute-start(f32[16,256]{1,0:T(8,128)S(1)} %get-tuple-element.66), channel_id=1, source_target_pairs={{0,16},{1,7},{2,18},{3,5},{4,20},{5,3},{6,22},{7,1},{8,24},{9,15},... | collective-permute-start | bytes 49160 | tf_op jit(solution)/shard_map/ppermute | solution.py:81
  49.8 5.5 %collective-permute-start.22 = (f32[16,256]{1,0:T(8,128)S(1)}, f32[16,256]{1,0:T(8,128)S(1)}, u32[]{:S(2)}, u32[]{:S(2)}) collective-permute-start(f32[16,256]{1,0:T(8,128)S(1)} %get-tuple-element.66), channel_id=1, source_target_pairs={{0,24},{1,5},{2,26},{3,7},{4,28},{5,1},{6,30},{7,3},{8,16},{9,13},... | collective-permute-start | bytes 49160 | tf_op jit(solution)/shard_map/ppermute | solution.py:81
  50.6 4.7 %collective-permute-start.21 = (f32[16,256]{1,0:T(8,128)S(1)}, f32[16,256]{1,0:T(8,128)S(1)}, u32[]{:S(2)}, u32[]{:S(2)}) collective-permute-start(f32[16,256]{1,0:T(8,128)S(1)} %get-tuple-element.66), channel_id=1, source_target_pairs={{0,8},{1,3},{2,10},{3,1},{4,12},{5,7},{6,14},{7,5},{8,0},{9,11},{1... | collective-permute-start | bytes 49160 | tf_op jit(solution)/shard_map/ppermute | solution.py:81
  59.1 6.9 %collective-permute-start.28 = (f32[8,256]{1,0:T(8,128)S(1)}, f32[8,256]{1,0:T(8,128)S(1)}, u32[]{:S(2)}, u32[]{:S(2)}) collective-permute-start(f32[8,256]{1,0:T(8,128)S(1)} %get-tuple-element.72.refs_0_), channel_id=1, source_target_pairs={{0,24},{8,16},{16,8},{24,0},{1,25},{9,17},{17,9},{25,1},{2,26},{10... | collective-permute-start | bytes 24584 | tf_op jit(solution)/shard_map/ppermute | solution.py:30
  61.2 4.9 %collective-permute-start.27 = (f32[8,256]{1,0:T(8,128)S(1)}, f32[8,256]{1,0:T(8,128)S(1)}, u32[]{:S(2)}, u32[]{:S(2)}) collective-permute-start(f32[8,256]{1,0:T(8,128)S(1)} %get-tuple-element.72.refs_0_), channel_id=1, source_target_pairs={{0,16},{8,24},{16,0},{24,8},{1,17},{9,25},{17,1},{25,9},{2,18},{10... | collective-permute-start | bytes 24584 | tf_op jit(solution)/shard_map/ppermute | solution.py:30
  61.2 4.9 %collective-permute-start.26 = (f32[8,256]{1,0:T(8,128)S(1)}, f32[8,256]{1,0:T(8,128)S(1)}, u32[]{:S(2)}, u32[]{:S(2)}) collective-permute-start(f32[8,256]{1,0:T(8,128)S(1)} %get-tuple-element.72.refs_0_), channel_id=1, source_target_pairs={{0,8},{8,0},{16,24},{24,16},{1,9},{9,1},{17,25},{25,17},{2,10},{10... | collective-permute-start | bytes 24584 | tf_op jit(solution)/shard_map/ppermute | solution.py:30
  73.1 6.5 %collective-permute-start.30 = (f32[272,128]{1,0:T(8,128)S(1)}, f32[272,128]{1,0:T(8,128)S(1)}, u32[]{:S(2)}, u32[]{:S(2)}) collective-permute-start(f32[272,128]{1,0:T(8,128)S(1)} %get-tuple-element.79), channel_id=1, source_target_pairs={{0,2},{1,3},{2,0},{3,1},{4,6},{5,7},{6,4},{7,5},{8,10},{9,11},{10,... | collective-permute-start | bytes 417800 | tf_op jit(solution)/shard_map/ppermute | solution.py:30
  75.3 8.4 %collective-permute-start.31 = (f32[272,128]{1,0:T(8,128)S(1)}, f32[272,128]{1,0:T(8,128)S(1)}, u32[]{:S(2)}, u32[]{:S(2)}) collective-permute-start(f32[272,128]{1,0:T(8,128)S(1)} %get-tuple-element.80), channel_id=1, source_target_pairs={{0,4},{1,5},{2,6},{3,7},{4,0},{5,1},{6,2},{7,3},{8,12},{9,13},{10,... | collective-permute-start | bytes 417800 | tf_op jit(solution)/shard_map/ppermute | solution.py:30
  75.3 8.4 %collective-permute-start.32 = (f32[272,128]{1,0:T(8,128)S(1)}, f32[272,128]{1,0:T(8,128)S(1)}, u32[]{:S(2)}, u32[]{:S(2)}) collective-permute-start(f32[272,128]{1,0:T(8,128)S(1)} %get-tuple-element.81), channel_id=1, source_target_pairs={{0,6},{1,7},{2,4},{3,5},{4,2},{5,3},{6,0},{7,1},{8,14},{9,15},{10,... | collective-permute-start | bytes 417800 | tf_op jit(solution)/shard_map/ppermute | solution.py:30
  (14 other events, 67.9 us)
where the time goes:
time: 85.6 us; the launch traced here: 84.8 us
  starting transfers between devices  31.4 us (37%)
  Pallas kernels  26.1 us (30%)
  waiting for transfers between devices  23.9 us (28%)
  local copies, waits for them, and re-layouts  2.46 us (3%)
  between operations  0.86 us (1%)
    ppermute x24, starting transfers between devices, swap(): lax.ppermute(part, axis, [(i, i ^ mask) for i in range(lax.axis_size(axis...  19.2 us
    ppermute x24, waiting for transfers between devices, swap(): lax.ppermute(part, axis, [(i, i ^ mask) for i in range(lax.axis_size(axis...  15.2 us
    ppermute x9, starting transfers between devices, swap_far(): return lax.ppermute(part, ('src', 'tgt'), pairs)  12.1 us
    ppermute x9, waiting for transfers between devices, swap_far(): return lax.ppermute(part, ('src', 'tgt'), pairs)  8.63 us
    pallas_call x1, Pallas kernels, on_device(): pl.pallas_call(functools.partial(first_kernel, x_parts, y_parts), out_sha...  5.1 us
    pallas_call x1, Pallas kernels, on_device(): pl.pallas_call(functools.partial(project_kernel, near), out_shape=(f32(tb...  4.33 us
    pallas_call x1, Pallas kernels, on_device(): pl.pallas_call(second_kernel, out_shape=(jax.ShapeDtypeStruct((nsrc, 2 *...  3.55 us
    pallas_call x1, Pallas kernels, on_device(): pl.pallas_call(functools.partial(shared_kernel, k % 2 ^ 1), out_shape=(f3...  3.33 us
  transfers between devices with their start and end apart: 33, of which 15 were waited for; matrix products, arithmetic and copies ran while one was open for 1% of the time, Pallas kernels for 11%

commit v1 on v0

--- a/solution.py
+++ b/solution.py
@@ -15,7 +15,7 @@
 LANES = 128
 FAR = (0, 1, 3, 2)
 GROUP = 16
-MOVE_GROUP = 6
+MOVE_GROUP = 8
 
 SMEM = pl.BlockSpec(memory_space=pltpu.SMEM)
 VMEM = pl.BlockSpec(memory_space=pltpu.VMEM)

time: 85.6 us -> 84.5 us (0.987); the launches traced: 84.8 us -> 85 us
  transfers between devices with their start and end apart: 33 -> 33, of which waited for: 15 -> 19; matrix products, arithmetic and copies ran while one was open for 1% -> 1% of each run, Pallas kernels for 11% -> 11%
where the time goes in v1:
time: 84.5 us; the launch traced here: 85 us
  starting transfers between devices  31.1 us (37%)
  Pallas kernels  26.3 us (31%)
  waiting for transfers between devices  24.2 us (29%)
  local copies, waits for them, and re-layouts  2.46 us (3%)
  between operations  0.86 us (1%)
    ppermute x24, starting transfers between devices, swap(): lax.ppermute(part, axis, [(i, i ^ mask) for i in range(lax.axis_size(axis...  19.4 us
    ppermute x24, waiting for transfers between devices, swap(): lax.ppermute(part, axis, [(i, i ^ mask) for i in range(lax.axis_size(axis...  15 us
    ppermute x9, starting transfers between devices, swap_far(): return lax.ppermute(part, ('src', 'tgt'), pairs)  11.7 us
    ppermute x9, waiting for transfers between devices, swap_far(): return lax.ppermute(part, ('src', 'tgt'), pairs)  9.16 us
    pallas_call x1, Pallas kernels, on_device(): pl.pallas_call(functools.partial(first_kernel, x_parts, y_parts), out_sha...  5.09 us
    pallas_call x1, Pallas kernels, on_device(): pl.pallas_call(functools.partial(project_kernel, near), out_shape=(f32(tb...  4.57 us
    pallas_call x1, Pallas kernels, on_device(): pl.pallas_call(second_kernel, out_shape=(jax.ShapeDtypeStruct((nsrc, 2 *...  3.54 us
    pallas_call x1, Pallas kernels, on_device(): pl.pallas_call(functools.partial(shared_kernel, k % 2 ^ 1), out_shape=(f3...  3.32 us
  transfers between devices with their start and end apart: 33, of which 19 were waited for; matrix products, arithmetic and copies ran while one was open for 1% of the time, Pallas kernels for 11%

profile of v1, /device:TPU:0, one launch (start us, length us, event | category | flops | bytes accessed | tf_op | source)
XLA Modules:
  0.0 85.0 jit_solution(7667897987285268680)
XLA Ops:
  0.6 1.7 %pack.1 = (bf16[272,128]{1,0:T(8,128)(2,1)}, bf16[528,128]{1,0:T(8,128)(2,1)}) custom-call(bf16[8,32,128]{2,1,0:T(8,128)(2,1)} %refs_0_.1, bf16[8,32]{1,0:T(8,128)(2,1)} %refs_1_.1, bf16[8,32]{1,0:T(8,128)(2,1)} %refs_2_.1, bf16[8,64,128]{2,1,0:T(8,128)(2,1)} %refs_3_.1, bf16[8,64]{1,0:T(8,128)(2,1)} %refs_4_.1, bf16[8,64]{1,0:T(8,128)(2,1)} %refs_5_.1), custom_call_target="tpu_custom_call" | custom-call | tf_op jit(solution)/shard_map/pack/pallas_call | solution.py:525
  2.4 5.1 %collective-permute-start.1 = (bf16[528,128]{1,0:T(8,128)(2,1)}, bf16[528,128]{1,0:T(8,128)(2,1)S(1)}, u32[]{:S(2)}, u32[]{:S(2)}) collective-permute-start(bf16[528,128]{1,0:T(8,128)(2,1)} %get-tuple-element.45.y_in_ref), channel_id=1, source_target_pairs={{0,24},{8,16},{16,8},{24,0},{1,25},{9,17},{17,9},{25,1},{2,26},{10... | collective-permute-start | bytes 405512 | tf_op jit(solution)/shard_map/ppermute | solution.py:30
  7.5 2.4 %collective-permute-start.4 = (bf16[272,128]{1,0:T(8,128)(2,1)}, bf16[272,128]{1,0:T(8,128)(2,1)S(1)}, u32[]{:S(2)}, u32[]{:S(2)}) collective-permute-start(bf16[272,128]{1,0:T(8,128)(2,1)} %get-tuple-element.44.x_in_ref), channel_id=1, source_target_pairs={{0,6},{1,7},{2,4},{3,5},{4,2},{5,3},{6,0},{7,1},{8,14},{9,15},{10,... | collective-permute-start | bytes 208904 | tf_op jit(solution)/shard_map/ppermute | solution.py:30
  11.0 2.0 %collective-permute-done.4.refs_3_ = bf16[272,128]{1,0:T(8,128)(2,1)S(1)} collective-permute-done((bf16[272,128]{1,0:T(8,128)(2,1)}, bf16[272,128]{1,0:T(8,128)(2,1)S(1)}, u32[]{:S(2)}, u32[]{:S(2)}) %collective-permute-start.4) | collective-permute-done | bytes 69664 | tf_op jit(solution)/shard_map/ppermute | solution.py:30
  17.3 1.4 %kept_pairs.1 = (s32[81]{0:T(128)S(1)}, bf16[272,128]{1,0:T(8,128)(2,1)S(1)}, bf16[528,128]{1,0:T(8,128)(2,1)S(1)}) custom-call(s32[8,8]{1,0:T(8,128)S(1)} %copy-done.2, s32[8]{0:T(128)S(1)} %copy-done.3, s32[8]{0:T(128)S(1)} %copy-done.4, bf16[272,128]{1,0:T(8,128)(2,1)S(1)} %copy-done.1, bf16[528,128]{1,0:T(8,128)(2,1)S(1)} %copy-done), custom_call_target="tpu_custom_call" | custom-call | tf_op jit(solution)/shard_map/kept_pairs/pallas_call | solution.py:536
  19.2 1.9 %collective-permute-done.9.refs_10_ = bf16[528,128]{1,0:T(8,128)(2,1)S(1)} collective-permute-done((bf16[528,128]{1,0:T(8,128)(2,1)}, bf16[528,128]{1,0:T(8,128)(2,1)S(1)}, u32[]{:S(2)}, u32[]{:S(2)}) %collective-permute-start.9) | collective-permute-done | bytes 135200 | tf_op jit(solution)/shard_map/ppermute | solution.py:30
  21.1 5.1 %first_sweep.1 = (bf16[8,8,32,128]{3,2,1,0:T(8,128)(2,1)S(1)}, bf16[4,8,64,128]{3,2,1,0:T(8,128)(2,1)S(1)}, f32[2,8,256]{2,1,0:T(8,128)S(1)}, f32[3,8,256]{2,1,0...) custom-call(s32[81]{0:T(128)S(1)} %get-tuple-element.46.list_ref, ...), custom_call_target="tpu_custom_call" | custom-call | tf_op jit(solution)/shard_map/first_sweep/pallas_call | solution.py:554
  27.6 2.3 %collective-permute-start.15 = (f32[16,256]{1,0:T(8,128)S(1)}, f32[16,256]{1,0:T(8,128)S(1)}, u32[]{:S(2)}, u32[]{:S(2)}) collective-permute-start(f32[16,256]{1,0:T(8,128)S(1)} %maximum_select_fusion), channel_id=1, source_target_pairs={{0,24},{1,5},{2,26},{3,7},{4,28},{5,1},{6,30},{7,3},{8,16},{9,13},... | collective-permute-start | bytes 49160 | tf_op jit(solution)/shard_map/ppermute | solution.py:81
  33.6 3.5 %second_sweep.1 = (bf16[4,16,64,128]{3,2,1,0:T(8,128)(2,1)S(1)}, f32[2,16,256]{2,1,0:T(8,128)S(1)}, f32[16,256]{1,0:T(8,128)S(1)}, f32[16,256]{1,0:T(8,128)S(1)}) custom-call(s32[81]{0:T(128)S(1)} %get-tuple-element.46.list_ref, s32[81]{0:T(128)S(1)} %collective-permute-done.10.list2_ref, bf16[8,8,32,128]{3,2,1,0:T(8,128)(2,1)S(1)} %get-tuple-element.55.x_ref, ...), custom_call_target="tpu_custom_call" | custom-call | tf_op jit(solution)/shard_map/second_sweep/pallas_call | solution.py:579
  37.2 2.4 %collective-permute-start.19 = (f32[16,256]{1,0:T(8,128)S(1)}, f32[16,256]{1,0:T(8,128)S(1)}, u32[]{:S(2)}, u32[]{:S(2)}) collective-permute-start(f32[16,256]{1,0:T(8,128)S(1)} %get-tuple-element.64), channel_id=1, source_target_pairs={{0,6},{1,17},{2,4},{3,19},{4,2},{5,21},{6,0},{7,23},{8,14},{9,25},... | collective-permute-start | bytes 49160 | tf_op jit(solution)/shard_map/ppermute | solution.py:81
  41.9 1.5 %collective-permute-done.18 = f32[16,256]{1,0:T(8,128)S(1)} collective-permute-done((f32[16,256]{1,0:T(8,128)S(1)}, f32[16,256]{1,0:T(8,128)S(1)}, u32[]{:S(2)}, u32[]{:S(2)}) %collective-permute-start.18) | collective-permute-done | bytes 16416 | tf_op jit(solution)/shard_map/ppermute | solution.py:81
  44.1 3.3 %sweep.1 = (f32[16,256]{1,0:T(8,128)S(1)}, f32[16,256]{1,0:T(8,128)S(1)}) custom-call(s32[81]{0:T(128)S(1)} %get-tuple-element.46.list_ref, s32[81]{0:T(128)S(1)} %collective-permute-done.10.list2_ref, bf16[8,8,32,128]{3,2,1,0:T(8,128)(2,1)S(1)} %get-tuple-element.55.x_ref, bf16[4,16,64,128]{3,2,1,0:T(8,128)(2,1)S(1)} %get-tuple-element.62.y_ref, ...), custom_call_target="tpu_custom_call" | custom-call | tf_op jit(solution)/shard_map/sweep/pallas_call | solution.py:594
  48.5 3.1 %collective-permute-start.22 = (f32[16,256]{1,0:T(8,128)S(1)}, f32[16,256]{1,0:T(8,128)S(1)}, u32[]{:S(2)}, u32[]{:S(2)}) collective-permute-start(f32[16,256]{1,0:T(8,128)S(1)} %get-tuple-element.66), channel_id=1, source_target_pairs={{0,24},{1,5},{2,26},{3,7},{4,28},{5,1},{6,30},{7,3},{8,16},{9,13},... | collective-permute-start | bytes 49160 | tf_op jit(solution)/shard_map/ppermute | solution.py:81
  52.1 2.0 %collective-permute-done.22 = f32[16,256]{1,0:T(8,128)S(1)} collective-permute-done((f32[16,256]{1,0:T(8,128)S(1)}, f32[16,256]{1,0:T(8,128)S(1)}, u32[]{:S(2)}, u32[]{:S(2)}) %collective-permute-start.22) | collective-permute-done | bytes 16416 | tf_op jit(solution)/shard_map/ppermute | solution.py:81
  56.7 2.5 %last_cols.1 = (f32[3,8,256]{2,1,0:T(8,128)S(1)}, f32[8,256]{1,0:T(8,128)S(1)}, f32[8,256]{1,0:T(8,128)S(1)}) custom-call(s32[81]{0:T(128)S(1)} %get-tuple-element.46.list_ref, bf16[8,8,32,128]{3,2,1,0:T(8,128)(2,1)S(1)} %get-tuple-element.55.x_ref, bf16[4,16,64,128]{3,2,1,0:T(8,128)(2,1)S(1)} %get-tuple-element.62.y_ref, ...), custom_call_target="tpu_custom_call" | custom-call | tf_op jit(solution)/shard_map/last_cols/pallas_call | solution.py:618
  60.4 3.2 %collective-permute-start.26 = (f32[8,256]{1,0:T(8,128)S(1)}, f32[8,256]{1,0:T(8,128)S(1)}, u32[]{:S(2)}, u32[]{:S(2)}) collective-permute-start(f32[8,256]{1,0:T(8,128)S(1)} %get-tuple-element.72.refs_0_), channel_id=1, source_target_pairs={{0,8},{8,0},{16,24},{24,16},{1,9},{9,1},{17,25},{25,17},{2,10},{10... | collective-permute-start | bytes 24584 | tf_op jit(solution)/shard_map/ppermute | solution.py:30
  63.6 2.5 %last_rows.1.rows_ref = f32[8,256]{1,0:T(8,128)S(1)} custom-call(s32[81]{0:T(128)S(1)} %get-tuple-element.46.list_ref, bf16[8,8,32,128]{3,2,1,0:T(8,128)(2,1)S(1)} %get-tuple-element.55.x_ref, bf16[4,16,64,128]{3,2,1,0:T(8,128)(2,1)S(1)} %get-tuple-element.62.y_ref, f32[3,8,256]{2,1,0:T(8,128)S(1)} %get-tuple-element.69.yfixed_ref), custom_call_target="tpu_custom_call" | custom-call | tf_op jit(solution)/shard_map/last_rows/pallas_call | solution.py:627
  66.1 4.6 %project.1 = (f32[8,256]{1,0:T(8,128)S(1)}, f32[4,272,128]{2,1,0:T(8,128)S(1)}, f32[4,272,128]{2,1,0:T(8,128)S(1)}) custom-call(s32[81]{0:T(128)S(1)} %get-tuple-element.46.list_ref, bf16[8,8,32,128]{3,2,1,0:T(8,128)(2,1)S(1)} %get-tuple-element.55.x_ref, bf16[4,16,64,128]{3,2,1,0:T(8,128)(2,1)S(1)} %get-tuple-element.62.y_ref, ...), custom_call_target="tpu_custom_call" | custom-call | tf_op jit(solution)/shard_map/project/pallas_call | solution.py:637
  70.8 1.9 %collective-permute-done.29.refs_1_ = f32[4,272,128]{2,1,0:T(8,128)S(1)} collective-permute-done((f32[4,272,128]{2,1,0:T(8,128)S(1)}, f32[4,272,128]{2,1,0:T(8,128)S(1)}, u32[]{:S(2)}, u32[]{:S(2)}) %collective-permute-start.29) | collective-permute-done | bytes 557088 | tf_op jit(solution)/shard_map/ppermute | solution.py:30
  73.4 2.5 %collective-permute-start.31 = (f32[272,128]{1,0:T(8,128)S(1)}, f32[272,128]{1,0:T(8,128)S(1)}, u32[]{:S(2)}, u32[]{:S(2)}) collective-permute-start(f32[272,128]{1,0:T(8,128)S(1)} %get-tuple-element.80), channel_id=1, source_target_pairs={{0,4},{1,5},{2,6},{3,7},{4,0},{5,1},{6,2},{7,3},{8,12},{9,13},{10,... | collective-permute-start | bytes 417800 | tf_op jit(solution)/shard_map/ppermute | solution.py:30
  75.9 1.4 %collective-permute-start.32 = (f32[272,128]{1,0:T(8,128)S(1)}, f32[272,128]{1,0:T(8,128)S(1)}, u32[]{:S(2)}, u32[]{:S(2)}) collective-permute-start(f32[272,128]{1,0:T(8,128)S(1)} %get-tuple-element.81), channel_id=1, source_target_pairs={{0,6},{1,7},{2,4},{3,5},{4,2},{5,3},{6,0},{7,1},{8,14},{9,15},{10,... | collective-permute-start | bytes 417800 | tf_op jit(solution)/shard_map/ppermute | solution.py:30
  78.0 2.0 %collective-permute-done.30.refs_1_ = f32[272,128]{1,0:T(8,128)S(1)} collective-permute-done((f32[272,128]{1,0:T(8,128)S(1)}, f32[272,128]{1,0:T(8,128)S(1)}, u32[]{:S(2)}, u32[]{:S(2)}) %collective-permute-start.30) | collective-permute-done | bytes 139296 | tf_op jit(solution)/shard_map/ppermute | solution.py:30
  79.9 2.2 %collective-permute-done.31.refs_2_ = f32[272,128]{1,0:T(8,128)S(1)} collective-permute-done((f32[272,128]{1,0:T(8,128)S(1)}, f32[272,128]{1,0:T(8,128)S(1)}, u32[]{:S(2)}, u32[]{:S(2)}) %collective-permute-start.31) | collective-permute-done | bytes 139296 | tf_op jit(solution)/shard_map/ppermute | solution.py:30
  82.2 1.8 %collective-permute-done.32.refs_3_ = f32[272,128]{1,0:T(8,128)S(1)} collective-permute-done((f32[272,128]{1,0:T(8,128)S(1)}, f32[272,128]{1,0:T(8,128)S(1)}, u32[]{:S(2)}, u32[]{:S(2)}) %collective-permute-start.32) | collective-permute-done | bytes 139296 | tf_op jit(solution)/shard_map/ppermute | solution.py:30
  (68 shorter events, 21.9 us)
Async XLA Ops:
  2.4 12.6 %collective-permute-start.1 = (bf16[528,128]{1,0:T(8,128)(2,1)}, bf16[528,128]{1,0:T(8,128)(2,1)S(1)}, u32[]{:S(2)}, u32[]{:S(2)}) collective-permute-start(bf16[528,128]{1,0:T(8,128)(2,1)} %get-tuple-element.45.y_in_ref), channel_id=1, source_target_pairs={{0,24},{8,16},{16,8},{24,0},{1,25},{9,17},{17,9},{25,1},{2,26},{10... | collective-permute-start | bytes 405512 | tf_op jit(solution)/shard_map/ppermute | solution.py:30
  7.5 7.5 %collective-permute-start = (bf16[528,128]{1,0:T(8,128)(2,1)}, bf16[528,128]{1,0:T(8,128)(2,1)S(1)}, u32[]{:S(2)}, u32[]{:S(2)}) collective-permute-start(bf16[528,128]{1,0:T(8,128)(2,1)} %get-tuple-element.45.y_in_ref), channel_id=1, source_target_pairs={{0,8},{8,0},{16,24},{24,16},{1,9},{9,1},{17,25},{25,17},{2,10},{10... | collective-permute-start | bytes 405512 | tf_op jit(solution)/shard_map/ppermute | solution.py:30
  7.5 5.5 %collective-permute-start.4 = (bf16[272,128]{1,0:T(8,128)(2,1)}, bf16[272,128]{1,0:T(8,128)(2,1)S(1)}, u32[]{:S(2)}, u32[]{:S(2)}) collective-permute-start(bf16[272,128]{1,0:T(8,128)(2,1)} %get-tuple-element.44.x_in_ref), channel_id=1, source_target_pairs={{0,6},{1,7},{2,4},{3,5},{4,2},{5,3},{6,0},{7,1},{8,14},{9,15},{10,... | collective-permute-start | bytes 208904 | tf_op jit(solution)/shard_map/ppermute | solution.py:30
  9.9 4.5 %collective-permute-start.3 = (bf16[272,128]{1,0:T(8,128)(2,1)}, bf16[272,128]{1,0:T(8,128)(2,1)S(1)}, u32[]{:S(2)}, u32[]{:S(2)}) collective-permute-start(bf16[272,128]{1,0:T(8,128)(2,1)} %get-tuple-element.44.x_in_ref), channel_id=1, source_target_pairs={{0,4},{1,5},{2,6},{3,7},{4,0},{5,1},{6,2},{7,3},{8,12},{9,13},{10,... | collective-permute-start | bytes 208904 | tf_op jit(solution)/shard_map/ppermute | solution.py:30
  10.4 4.5 %collective-permute-start.2 = (bf16[272,128]{1,0:T(8,128)(2,1)}, bf16[272,128]{1,0:T(8,128)(2,1)S(1)}, u32[]{:S(2)}, u32[]{:S(2)}) collective-permute-start(bf16[272,128]{1,0:T(8,128)(2,1)} %get-tuple-element.44.x_in_ref), channel_id=1, source_target_pairs={{0,2},{1,3},{2,0},{3,1},{4,6},{5,7},{6,4},{7,5},{8,10},{9,11},{10,... | collective-permute-start | bytes 208904 | tf_op jit(solution)/shard_map/ppermute | solution.py:30
  13.0 8.1 %collective-permute-start.9 = (bf16[528,128]{1,0:T(8,128)(2,1)}, bf16[528,128]{1,0:T(8,128)(2,1)S(1)}, u32[]{:S(2)}, u32[]{:S(2)}) collective-permute-start(bf16[528,128]{1,0:T(8,128)(2,1)} %get-tuple-element.45.y_in_ref), channel_id=1, source_target_pairs={{0,16},{8,24},{16,0},{24,8},{1,17},{9,25},{17,1},{25,9},{2,18},{10... | collective-permute-start | bytes 405512 | tf_op jit(solution)/shard_map/ppermute | solution.py:30
  14.4 4.3 %collective-permute-start.5 = (bf16[272,128]{1,0:T(8,128)(2,1)}, bf16[272,128]{1,0:T(8,128)(2,1)S(1)}, u32[]{:S(2)}, u32[]{:S(2)}) collective-permute-start(bf16[272,128]{1,0:T(8,128)(2,1)} %get-tuple-element.44.x_in_ref), channel_id=1, source_target_pairs={{0,1},{1,0},{2,3},{3,2},{4,5},{5,4},{6,7},{7,6},{8,9},{9,8},{10,11... | collective-permute-start | bytes 208904 | tf_op jit(solution)/shard_map/ppermute | solution.py:30
  15.0 6.1 %collective-permute-start.6 = (bf16[272,128]{1,0:T(8,128)(2,1)S(1)}, bf16[272,128]{1,0:T(8,128)(2,1)S(1)}, u32[]{:S(2)}, u32[]{:S(2)}) collective-permute-start(bf16[272,128]{1,0:T(8,128)(2,1)S(1)} %collective-permute-done.2.refs_1_), channel_id=1, source_target_pairs={{0,1},{1,0},{2,3},{3,2},{4,5},{5,4},{6,7},{7,6},{8,9},{9,8},{10,11... | collective-permute-start | bytes 208904 | tf_op jit(solution)/shard_map/ppermute | solution.py:30
  15.0 6.1 %collective-permute-start.7 = (bf16[272,128]{1,0:T(8,128)(2,1)S(1)}, bf16[272,128]{1,0:T(8,128)(2,1)S(1)}, u32[]{:S(2)}, u32[]{:S(2)}) collective-permute-start(bf16[272,128]{1,0:T(8,128)(2,1)S(1)} %collective-permute-done.3.refs_2_), channel_id=1, source_target_pairs={{0,1},{1,0},{2,3},{3,2},{4,5},{5,4},{6,7},{7,6},{8,9},{9,8},{10,11... | collective-permute-start | bytes 208904 | tf_op jit(solution)/shard_map/ppermute | solution.py:30
  15.5 5.6 %collective-permute-start.8 = (bf16[272,128]{1,0:T(8,128)(2,1)S(1)}, bf16[272,128]{1,0:T(8,128)(2,1)S(1)}, u32[]{:S(2)}, u32[]{:S(2)}) collective-permute-start(bf16[272,128]{1,0:T(8,128)(2,1)S(1)} %collective-permute-done.4.refs_3_), channel_id=1, source_target_pairs={{0,1},{1,0},{2,3},{3,2},{4,5},{5,4},{6,7},{7,6},{8,9},{9,8},{10,11... | collective-permute-start | bytes 208904 | tf_op jit(solution)/shard_map/ppermute | solution.py:30
  18.7 7.5 %collective-permute-start.10 = (s32[81]{0:T(128)S(1)}, s32[81]{0:T(128)S(1)}, u32[]{:S(2)}, u32[]{:S(2)}) collective-permute-start(s32[81]{0:T(128)S(1)} %get-tuple-element.46.list_ref), channel_id=1, source_target_pairs={{0,1},{1,0},{2,3},{3,2},{4,5},{5,4},{6,7},{7,6},{8,9},{9,8},{10,11... | collective-permute-start | bytes 980 | tf_op jit(solution)/shard_map/ppermute | solution.py:30
  26.3 7.3 %collective-permute-start.11 = (bf16[4,8,64,128]{3,2,1,0:T(8,128)(2,1)S(1)}, bf16[4,8,64,128]{3,2,1,0:T(8,128)(2,1)S(1)}, u32[]{:S(2)}, u32[]{:S(2)}) collective-permute-start(bf16[4,8,64,128]{3,2,1,0:T(8,128)(2,1)S(1)} %get-tuple-element.58.y1_ref), channel_id=1, source_target_pairs={{0,1},{1,0},{2,3},{3,2},{4,5},{5,4},{6,7},{7,6},{8,9},{9,8},{10,11... | collective-permute-start | bytes 1572872 | tf_op jit(solution)/shard_map/ppermute | solution.py:30
  27.5 4.7 %collective-permute-start.16 = (f32[16,256]{1,0:T(8,128)S(1)}, f32[16,256]{1,0:T(8,128)S(1)}, u32[]{:S(2)}, u32[]{:S(2)}) collective-permute-start(f32[16,256]{1,0:T(8,128)S(1)} %maximum_select_fusion), channel_id=1, source_target_pairs={{0,16},{1,7},{2,18},{3,5},{4,20},{5,3},{6,22},{7,1},{8,24},{9,15},... | collective-permute-start | bytes 49160 | tf_op jit(solution)/shard_map/ppermute | solution.py:81
  27.6 5.6 %collective-permute-start.15 = (f32[16,256]{1,0:T(8,128)S(1)}, f32[16,256]{1,0:T(8,128)S(1)}, u32[]{:S(2)}, u32[]{:S(2)}) collective-permute-start(f32[16,256]{1,0:T(8,128)S(1)} %maximum_select_fusion), channel_id=1, source_target_pairs={{0,24},{1,5},{2,26},{3,7},{4,28},{5,1},{6,30},{7,3},{8,16},{9,13},... | collective-permute-start | bytes 49160 | tf_op jit(solution)/shard_map/ppermute | solution.py:81
  37.2 4.7 %collective-permute-start.19 = (f32[16,256]{1,0:T(8,128)S(1)}, f32[16,256]{1,0:T(8,128)S(1)}, u32[]{:S(2)}, u32[]{:S(2)}) collective-permute-start(f32[16,256]{1,0:T(8,128)S(1)} %get-tuple-element.64), channel_id=1, source_target_pairs={{0,6},{1,17},{2,4},{3,19},{4,2},{5,21},{6,0},{7,23},{8,14},{9,25},... | collective-permute-start | bytes 49160 | tf_op jit(solution)/shard_map/ppermute | solution.py:81
  47.4 4.7 %collective-permute-start.23 = (f32[16,256]{1,0:T(8,128)S(1)}, f32[16,256]{1,0:T(8,128)S(1)}, u32[]{:S(2)}, u32[]{:S(2)}) collective-permute-start(f32[16,256]{1,0:T(8,128)S(1)} %get-tuple-element.66), channel_id=1, source_target_pairs={{0,16},{1,7},{2,18},{3,5},{4,20},{5,3},{6,22},{7,1},{8,24},{9,15},... | collective-permute-start | bytes 49160 | tf_op jit(solution)/shard_map/ppermute | solution.py:81
  48.5 5.5 %collective-permute-start.22 = (f32[16,256]{1,0:T(8,128)S(1)}, f32[16,256]{1,0:T(8,128)S(1)}, u32[]{:S(2)}, u32[]{:S(2)}) collective-permute-start(f32[16,256]{1,0:T(8,128)S(1)} %get-tuple-element.66), channel_id=1, source_target_pairs={{0,24},{1,5},{2,26},{3,7},{4,28},{5,1},{6,30},{7,3},{8,16},{9,13},... | collective-permute-start | bytes 49160 | tf_op jit(solution)/shard_map/ppermute | solution.py:81
  51.6 3.9 %collective-permute-start.25 = (f32[16,256]{1,0:T(8,128)S(1)}, f32[16,256]{1,0:T(8,128)S(1)}, u32[]{:S(2)}, u32[]{:S(2)}) collective-permute-start(f32[16,256]{1,0:T(8,128)S(1)} %get-tuple-element.67.refs_2_), channel_id=1, source_target_pairs={{0,1},{1,0},{2,3},{3,2},{4,5},{5,4},{6,7},{7,6},{8,9},{9,8},{10,11... | collective-permute-start | bytes 49160 | tf_op jit(solution)/shard_map/ppermute | solution.py:30
  59.1 6.9 %collective-permute-start.28 = (f32[8,256]{1,0:T(8,128)S(1)}, f32[8,256]{1,0:T(8,128)S(1)}, u32[]{:S(2)}, u32[]{:S(2)}) collective-permute-start(f32[8,256]{1,0:T(8,128)S(1)} %get-tuple-element.72.refs_0_), channel_id=1, source_target_pairs={{0,24},{8,16},{16,8},{24,0},{1,25},{9,17},{17,9},{25,1},{2,26},{10... | collective-permute-start | bytes 24584 | tf_op jit(solution)/shard_map/ppermute | solution.py:30
  60.0 6.1 %collective-permute-start.27 = (f32[8,256]{1,0:T(8,128)S(1)}, f32[8,256]{1,0:T(8,128)S(1)}, u32[]{:S(2)}, u32[]{:S(2)}) collective-permute-start(f32[8,256]{1,0:T(8,128)S(1)} %get-tuple-element.72.refs_0_), channel_id=1, source_target_pairs={{0,16},{8,24},{16,0},{24,8},{1,17},{9,25},{17,1},{25,9},{2,18},{10... | collective-permute-start | bytes 24584 | tf_op jit(solution)/shard_map/ppermute | solution.py:30
  60.4 5.7 %collective-permute-start.26 = (f32[8,256]{1,0:T(8,128)S(1)}, f32[8,256]{1,0:T(8,128)S(1)}, u32[]{:S(2)}, u32[]{:S(2)}) collective-permute-start(f32[8,256]{1,0:T(8,128)S(1)} %get-tuple-element.72.refs_0_), channel_id=1, source_target_pairs={{0,8},{8,0},{16,24},{24,16},{1,9},{9,1},{17,25},{25,17},{2,10},{10... | collective-permute-start | bytes 24584 | tf_op jit(solution)/shard_map/ppermute | solution.py:30
  73.4 6.6 %collective-permute-start.30 = (f32[272,128]{1,0:T(8,128)S(1)}, f32[272,128]{1,0:T(8,128)S(1)}, u32[]{:S(2)}, u32[]{:S(2)}) collective-permute-start(f32[272,128]{1,0:T(8,128)S(1)} %get-tuple-element.79), channel_id=1, source_target_pairs={{0,2},{1,3},{2,0},{3,1},{4,6},{5,7},{6,4},{7,5},{8,10},{9,11},{10,... | collective-permute-start | bytes 417800 | tf_op jit(solution)/shard_map/ppermute | solution.py:30
  73.4 8.7 %collective-permute-start.31 = (f32[272,128]{1,0:T(8,128)S(1)}, f32[272,128]{1,0:T(8,128)S(1)}, u32[]{:S(2)}, u32[]{:S(2)}) collective-permute-start(f32[272,128]{1,0:T(8,128)S(1)} %get-tuple-element.80), channel_id=1, source_target_pairs={{0,4},{1,5},{2,6},{3,7},{4,0},{5,1},{6,2},{7,3},{8,12},{9,13},{10,... | collective-permute-start | bytes 417800 | tf_op jit(solution)/shard_map/ppermute | solution.py:30
  75.9 8.1 %collective-permute-start.32 = (f32[272,128]{1,0:T(8,128)S(1)}, f32[272,128]{1,0:T(8,128)S(1)}, u32[]{:S(2)}, u32[]{:S(2)}) collective-permute-start(f32[272,128]{1,0:T(8,128)S(1)} %get-tuple-element.81), channel_id=1, source_target_pairs={{0,6},{1,7},{2,4},{3,5},{4,2},{5,3},{6,0},{7,1},{8,14},{9,15},{10,... | collective-permute-start | bytes 417800 | tf_op jit(solution)/shard_map/ppermute | solution.py:30
  (14 other events, 68.0 us)
